TPU v7x, 256 devices: a whole 4x4x8 slice. The times are simulated.
256 devices in a mesh: blk: 64 (over x_lo, y, z), tower: 4 (over x_hi, core).
Axes of the slice: x: 4 (x_hi: 2, x_lo: 2; x = x_hi * 2 + x_lo), y: 4, z: 8, core: 2. Of those that a mesh axis runs over, the one named last changes fastest.
Arguments:
- layer_input: bfloat16 [131072, 1152], P(('blk', 'tower')), may hold values from -8 to 8
- caption_ids: int32 [512, 64], P('blk'), may hold values from 0 to 31999, as said below
- positives: int32 [384], P('blk'), may hold values from 0 to 511, as said below
- ln_gain: float32 [2, 1152], replicated, may hold values from 0.1 to 1.9
- w_first: bfloat16 [2, 1152, 2176], P(None, None, 'blk'), may hold values from -0.1875 to 0.1875
- w_second: bfloat16 [2, 2176, 1152], P(None, 'blk'), may hold values from -0.125 to 0.125
- logit_scale: float32 [1], replicated, may hold values from 20 to 80
- logit_bias: float32 [1], replicated, may hold values from -6 to -2
Outputs:
- input_grad: float32 [131072, 1152], P(('blk', 'tower'))
Inputs may be any that keep to these rules, and one draw needn't show every extreme that they name: `caption_ids`: each caption's ids are nonzero for its first 32 or more positions and zero after; some caption has no zeros. `positives`: no two images have the same positive caption.
All inputs are finite; a program needn't handle non-finite values.
Results may differ from a plain program's by a relative error of at most 0.013.
Values may be sent and summed in bfloat16 or wider, within the bound.
A program may use at most 128 MiB of HBM per device.

v0:
```python
import jax
import jax.numpy as jnp
from jax import lax
from jax.sharding import PartitionSpec as P

PATCHES = 256
TEXT_LEN = 64


norm_eps = 1e-06
loss_scale = 128.0
gelu_coeff = 0.7978845608028654


def broadcast(value, axis, source):
    kept = jnp.where(lax.axis_index(axis) == source, value, 0).astype(value.dtype)
    return lax.psum(kept, axis)


def gelu_pair(pre):
    inner = gelu_coeff * (pre + 0.044715 * pre * pre * pre)
    tanh_part = jnp.tanh(inner)
    value = 0.5 * pre * (1.0 + tanh_part)
    slope = 0.5 * (1.0 + tanh_part) + 0.5 * pre * (1.0 - tanh_part * tanh_part) * gelu_coeff * (
        1.0 + 3.0 * 0.044715 * pre * pre
    )
    return (value, slope)


def contract_last(left, right):
    return lax.dot_general(
        left, right, (((1,), (1,)), ((), ())), preferred_element_type=jnp.float32
    )


def contract_first(left, right):
    return lax.dot_general(
        left, right, (((0,), (0,)), ((), ())), preferred_element_type=jnp.float32
    )


def unit_rows(pooled):
    norm = jnp.sqrt(jnp.sum(pooled * pooled, axis=-1, keepdims=True) + norm_eps)
    return (pooled / norm, norm)


def unit_back(unit, norm, grad_emb):
    return (grad_emb - unit * jnp.sum(unit * grad_emb, axis=-1, keepdims=True)) / norm


def body(layer_input, caption_ids, positives, ln_gain, w_first, w_second, logit_scale, logit_bias):
    groups = lax.axis_size("tower")
    tower_index = lax.axis_index("tower")
    is_text = tower_index == groups - 1
    image_weight = jnp.where(is_text, 0.0, 1.0).astype(jnp.float32)
    row_count, width = layer_input.shape
    cap_count = caption_ids.shape[0]
    img_count = positives.shape[0] // (groups - 1)
    gain = jnp.where(is_text, ln_gain[1], ln_gain[0])
    first = jnp.where(is_text, w_first[1], w_first[0])
    second = jnp.where(is_text, w_second[1], w_second[0])
    values = layer_input.astype(jnp.float32)
    centered = values - jnp.mean(values, axis=-1, keepdims=True)
    variance = jnp.mean(centered * centered, axis=-1, keepdims=True)
    inv_std = lax.rsqrt(variance + norm_eps)
    standard = centered * inv_std
    normed = (standard * gain).astype(jnp.bfloat16)
    pre = jnp.dot(
        normed, lax.all_gather(first, "blk", axis=1, tiled=True), preferred_element_type=jnp.float32
    )
    value, slope = gelu_pair(pre)
    hidden = value.astype(jnp.bfloat16)
    columns = hidden
    block_out = values + jnp.dot(
        columns,
        lax.all_gather(second, "blk", axis=0, tiled=True),
        preferred_element_type=jnp.float32,
    )
    image_pool = jnp.mean(block_out.reshape(img_count, PATCHES, width), axis=1)
    mask = (caption_ids != 0).astype(jnp.float32)
    counts = jnp.sum(mask, axis=1, keepdims=True)
    text_pool = (
        jnp.sum(block_out.reshape(cap_count, TEXT_LEN, width) * mask[:, :, None], axis=1) / counts
    )
    image_unit, image_norm = unit_rows(image_pool)
    text_unit, text_norm = unit_rows(text_pool)
    image_emb = image_unit.astype(jnp.bfloat16)
    text_emb = text_unit.astype(jnp.bfloat16)
    span = broadcast(text_emb, "tower", groups - 1)
    slot = jnp.minimum(tower_index, groups - 2) * img_count
    own_positive = lax.dynamic_slice_in_dim(positives, slot, img_count, 0)
    scale = logit_scale[0]
    bias = logit_bias[0]
    every = lax.all_gather(span, "blk", axis=0, tiled=True)
    logits = scale * contract_last(image_emb, every) + bias
    caption_index = jnp.arange(every.shape[0], dtype=jnp.int32)
    onehot = (own_positive[:, None] == caption_index[None, :]).astype(jnp.float32)
    coef = (loss_scale * (jax.nn.sigmoid(logits) - onehot) * image_weight).astype(jnp.bfloat16)
    grad_image = scale * jnp.dot(coef, every, preferred_element_type=jnp.float32)
    span_grad = lax.psum_scatter(
        scale * contract_first(coef, image_emb), "blk", scatter_dimension=0, tiled=True
    )
    grad_text = lax.psum(span_grad.astype(jnp.bfloat16), "tower").astype(jnp.float32)
    image_gp = unit_back(image_unit, image_norm, grad_image)
    text_gp = unit_back(text_unit, text_norm, grad_text)
    image_rows = jnp.broadcast_to(
        image_gp[:, None, :] / PATCHES, (img_count, PATCHES, width)
    ).reshape(row_count, width)
    text_rows = (text_gp[:, None, :] * (mask / counts)[:, :, None]).reshape(row_count, width)
    grad_out = jnp.where(is_text, text_rows, image_rows)
    grad_rows = grad_out.astype(jnp.bfloat16)
    grad_hidden = contract_last(grad_rows, lax.all_gather(second, "blk", axis=0, tiled=True))
    grad_pre = (grad_hidden * slope).astype(jnp.bfloat16)
    columns = grad_pre
    grad_normed = contract_last(columns, lax.all_gather(first, "blk", axis=1, tiled=True))
    grad_std = grad_normed * gain
    first_mean = jnp.mean(grad_std, axis=-1, keepdims=True)
    second_mean = jnp.mean(grad_std * standard, axis=-1, keepdims=True)
    return grad_out + inv_std * (grad_std - first_mean - standard * second_mean)


def solution(mesh):
    placed = (
        P(("blk", "tower"), None),
        P("blk", None),
        P("blk"),
        P(),
        P(None, None, "blk"),
        P(None, "blk", None),
        P(),
        P(),
    )
    return jax.shard_map(
        body, mesh=mesh, in_specs=placed, out_specs=P(("blk", "tower"), None), check_vma=False
    )
```

profile of v0, /device:TPU:1, one launch (start us, length us, event | category | flops | bytes accessed | tf_op | source)
XLA Modules:
  0.0 1350.8 jit_solution(4066292563292867976)
XLA Ops:
  6.5 2.0 broadcast_select_fusion.1
  8.6 1.9 broadcast_select_fusion
  10.6 0.8 fusion.67
  11.5 0.8 fusion.54
  12.3 1.5 convert_reduce_fusion
  14.3 277.5 %all-gather.8.cloned.1.call-done = bf16[1,1152,2176]{1,0,2:T(2,128)(2,1)} async-done(((bf16[1,1152,34]{1,0,2:T(2,128)(2,1)}), bf16[1,1152,2176]{1,0,2:T(2,128)(2,1)}) %all-gather.8.cloned.1.call-update) | async-done | bytes 5013520 | tf_op jit(solution)/shard_map/all_gather | solution.py:69
  291.8 22.1 %copy.13 = bf16[1,1152,2176]{2,1,0:T(8,128)(2,1)} copy(bf16[1,1152,2176]{1,0,2:T(2,128)(2,1)} %all-gather.8.cloned.1.call-done) | data formatting | bytes 10027008 | tf_op jit(solution)/shard_map/all_gather | solution.py:69
  313.9 7.6 fusion.5
  321.5 287.1 %all-gather.10.cloned.1.call-done = bf16[1,2176,1152]{2,0,1:T(2,128)(2,1)} async-done(((bf16[1,34,1152]{2,0,1:T(2,128)(2,1)}), bf16[1,2176,1152]{2,0,1:T(2,128)(2,1)}) %all-gather.10.cloned.1.call-update) | async-done | bytes 5013520 | tf_op jit(solution)/shard_map/all_gather | solution.py:76
  608.6 9.2 multiply_reduce_fusion
  618.0 0.6 add_sqrt_fusion
  618.6 0.5 copy-done.8
  619.1 0.7 convert_select_fusion
  619.8 53.2 %psum.14 = bf16[8,1152]{1,0:T(8,128)(2,1)} all-reduce(bf16[8,1152]{1,0:T(8,128)(2,1)} %convert_select_fusion), channel_id=1, replica_groups=mesh['blk'=64,'tower'=4] {'tower'}, use_global_device_ids=true, to_apply=%region_7.8 | all-reduce | flops 9216 | bytes 36864 | tf_op jit(solution)/shard_map/psum | solution.py:17
  674.5 1.3 dynamic_slice.3
  675.8 1.3 dynamic-slice
  678.1 247.1 %all-gather.6.cloned.1.call-done = bf16[512,1152]{1,0:T(8,128)(2,1)} async-done(((bf16[8,1152]{1,0:T(8,128)(2,1)}), bf16[512,1152]{1,0:T(8,128)(2,1)}) %all-gather.6.cloned.1.call-update) | async-done | bytes 1179664 | tf_op jit(solution)/shard_map/all_gather | solution.py:94
  925.2 1.7 fusion.51
  926.9 0.5 copy-done.7
  927.4 1.2 convolution_multiply_fusion.1
  928.6 279.4 %all-reduce.2 = bf16[512,1152]{1,0:T(8,128)(2,1)} all-reduce(f32[512,1152]{1,0:T(8,128)S(1)} %convolution_multiply_fusion.1), channel_id=4, replica_groups=mesh['blk'=64,'tower'=4] {'blk'}, use_global_device_ids=true, to_apply=%region_8.9.clone | all-reduce | flops 589824 | bytes 3538944
  1208.0 0.7 dynamic-slice_convert_fusion
  1208.7 111.0 %psum.15 = bf16[8,1152]{1,0:T(8,128)(2,1)S(1)} all-reduce(bf16[8,1152]{1,0:T(8,128)(2,1)S(1)} %dynamic-slice_convert_fusion), channel_id=1, replica_groups=mesh['blk'=64,'tower'=4] {'tower'}, use_global_device_ids=true, to_apply=%region_9.10 | all-reduce | flops 9216 | bytes 36864 | tf_op jit(solution)/shard_map/psum | solution.py:103
  1319.7 1.0 fusion.52
  1320.7 1.6 multiply_reduce_fusion.2
  1322.4 0.7 divide_multiply_fusion
  1323.1 0.9 fusion.53
  1324.0 0.6 copy-done.2
  1324.6 1.3 fusion.31
  1325.9 14.7 %fusion.68 = (f32[512]{0:T(512)}, f32[512]{0:T(512)}, f32[512,1152]{1,0:T(8,128)S(1)}) fusion(f32[512]{0:T(512)} %copy-done.9, f32[512]{0:T(512)} %copy-done.6, bf16[512,1152]{1,0:T(8,128)(2,1)S(1)} %copy-done, f32[1152]{0:T(1024)} %copy-done.10, bf16[1,1152,2176]{2,1,0:T(8,128)(2,1)} %copy.13, bf16[512,1152]{1,0:T(8,128)(2,1)} %fusion.31, ...), kind=kOutput, calls=%fused_computation.95 | convolution fusion | flops 5159123968 | bytes 19214848 | tf_op jit(solution)/shard_map/dot_general | solution.py:31
  1340.6 0.6 broadcast_multiply_fusion
  1341.3 3.0 fusion.29
  (37 shorter events, 1.3 us)
Async XLA Ops:
  6.5 7.7 copy-start.5
  6.5 7.2 copy-start
  6.5 285.2 %all-gather.8.cloned.1.call-start = ((), (), s32[]{:S(2)}) async-start(), calls=%async_computation.1 | async-start | bytes 10183680 | tf_op jit(solution)/shard_map/all_gather | solution.py:69
  8.6 600.0 %all-gather.10.cloned.1.call-start = ((), (), s32[]{:S(2)}) async-start(), calls=%async_computation.2 | async-start | bytes 10183680 | tf_op jit(solution)/shard_map/all_gather | solution.py:76
  10.6 914.6 %all-gather.6.cloned.1.call-start = ((), (), s32[]{:S(2)}) async-start(), calls=%async_computation | async-start | bytes 1198080 | tf_op jit(solution)/shard_map/all_gather | solution.py:94
  12.3 301.6 %copy-start.10 = (f32[1152]{0:T(1024)}, f32[1152]{0:T(1024)S(1)}, u32[]{:S(2)}) copy-start(f32[1152]{0:T(1024)S(1)} %fusion.54) | copy-start | bytes 13828
  13.8 300.1 %copy-start.6 = (f32[512]{0:T(512)}, f32[512]{0:T(512)S(1)}, u32[]{:S(2)}) copy-start(f32[512]{0:T(512)S(1)} %broadcast_multiply_fusion.2) | copy-start | bytes 6148
  14.3 299.6 %copy-start.9 = (f32[512]{0:T(512)}, f32[512]{0:T(512)S(1)}, u32[]{:S(2)}) copy-start(f32[512]{0:T(512)S(1)} %add_rsqrt_fusion) | copy-start | bytes 6148
  617.8 0.8 copy-start.1
  618.6 0.5 copy-start.8
  678.1 248.8 %copy-start.11 = (f32[2]{0:T(128)}, f32[2]{0:T(128)S(1)}, u32[]{:S(2)}) copy-start(f32[2]{0:T(128)S(1)} %add_sqrt_fusion.1) | copy-start | bytes 28
  926.9 0.5 copy-start.7
  1323.1 0.9 copy-start.3
  1324.0 0.6 copy-start.2
  1325.9 15.4 %copy-start.4 = (f32[2,1152]{1,0:T(2,128)S(1)}, f32[2,1152]{1,0:T(2,128)}, u32[]{:S(2)}) copy-start(f32[2,1152]{1,0:T(2,128)} %copy-done.3) | copy-start | bytes 27652
Sparse Core Ops, SparseCore 0:
  9.2 282.5 all-gather.7
  293.6 314.9 all-gather.9
  673.2 251.9 all-gather.5
where the time goes:
time: 1350 us
  waiting for transfers between devices  812 us (60%)
  blocking collectives  444 us (33%)
  matrix products  36.1 us (3%)
  local copies, waits for them, and re-layouts  27.2 us (2%)
  other arithmetic  16.8 us (1%)
  between operations  15.2 us (1%)
    all_gather x1, waiting for transfers between devices, body(): lax.all_gather(second, 'blk', axis=0, tiled=True)  287 us
    unnamed x1, blocking collectives  279 us
    all_gather x1, waiting for transfers between devices, body(): lax.all_gather(first, 'blk', axis=1, tiled=True)  278 us
    all_gather x1, waiting for transfers between devices, body(): every = lax.all_gather(span, 'blk', axis=0, tiled=True)  247 us
    psum x1, blocking collectives, body(): lax.psum(span_grad.astype(jnp.bfloat16), 'tower').astype(jnp.float32)  111 us
    psum x1, blocking collectives, broadcast(): return lax.psum(kept, axis)  53.2 us
  transfers between devices with their start and end apart: 3, of which 3 were waited for; matrix products, arithmetic and copies ran while one was open for 3% of the time, Pallas kernels for 0%

commit v1 on v0

v1 whole, which is shorter than its diff:
```python
import functools

import jax
import jax.numpy as jnp
from jax import lax
from jax.experimental import pallas as pl
from jax.experimental.pallas import tpu as pltpu
from jax.sharding import PartitionSpec as P

D = 1152
ROWS = 512
N_Y = 4
N_Z = 8
MAIN = 32
GROUP = N_Z * MAIN
EXTRA = 16
SEG = 64
LANES = 128
KEYED = D + LANES

norm_eps = 1e-06
loss_scale = 128.0
gelu_c = 0.7978845608028654
gelu_k = gelu_c * 0.044715

MESH = pl.DeviceIdType.MESH
bf16 = jnp.bfloat16
f32 = jnp.float32


def dot_nt(left, right):
    return lax.dot_general(left, right, (((1,), (1,)), ((), ())), preferred_element_type=f32)


def dot_nn(left, right):
    return jnp.dot(left, right, preferred_element_type=f32)


def device_of(x, y, z, core):
    x = lax.rem(x + 8, 4)
    y = lax.rem(y + 8, N_Y)
    z = lax.rem(z + 16, N_Z)
    return (lax.rem(x, 2) * (N_Y * N_Z) + y * N_Z + z, (x // 2) * 2 + core)


def normalise(rows):
    values = rows.astype(f32)
    centered = values - jnp.mean(values, axis=-1, keepdims=True)
    variance = jnp.mean(centered * centered, axis=-1, keepdims=True)
    inv_std = lax.rsqrt(variance + norm_eps)
    return centered * inv_std, inv_std


def kernel(
    x_ref, rowmask_ref, pmask_ref, count_ref, key_ref, gain_ref, w1_ref, w2_ref, scale_ref, bias_ref,
    out_ref,
    wa, wb, ea, eb, exa, exb, normed, pre, slope, slope_e, pooled, pooled_e, acc,
    tile, column, bundle, others, part, gsum, gpre,
    recv_main, recv_ex, recv_e, send_zm, send_ze, send_ym, send_ye, send_xm, send_xe,
    c_send, c_recv, o_send, o_recv, g_send, g_recv,
):
    blk = lax.axis_index("blk")
    tower = lax.axis_index("tower")
    x_lo = blk // (N_Y * N_Z)
    y = lax.rem(blk // N_Z, N_Y)
    z = lax.rem(blk, N_Z)
    x_hi = tower // 2
    core = lax.rem(tower, 2)
    x = x_hi * 2 + x_lo
    is_text = tower == 3
    t = jnp.where(is_text, 1, 0)
    role = x * 2 + core
    gid = x_lo * N_Y + y

    toward = jnp.where(core == 1, 1 - 2 * x_lo, 2 * x_lo - 1)
    partner = device_of(x + toward, y, z, core)

    def ring_z(d):
        return device_of(x, y, z + d, core)

    def ring_y(d):
        return device_of(x, y + d, z, core)

    def in_column(d):
        q = lax.rem(role + d, 8)
        return device_of(q // 2, y, z, lax.rem(q, 2))

    barrier = pltpu.get_barrier_semaphore()
    for d in range(1, N_Z):
        pl.semaphore_signal(barrier, inc=1, device_id=ring_z(d), device_id_type=MESH)
    for d in range(1, N_Y):
        pl.semaphore_signal(barrier, inc=1, device_id=ring_y(d), device_id_type=MESH)
    for d in range(1, 8):
        pl.semaphore_signal(barrier, inc=1, device_id=in_column(d), device_id_type=MESH)
    for d in range(1, N_Y):
        pl.semaphore_signal(barrier, inc=1, device_id=device_of(x, y - d, z + role, core), device_id_type=MESH)

    @pl.when(role != 0)
    def _():
        pl.semaphore_signal(barrier, inc=1, device_id=device_of(x, y, z + role, core), device_id_type=MESH)

    row = lax.broadcasted_iota(jnp.int32, (MAIN + EXTRA, 34), 0)
    col = lax.broadcasted_iota(jnp.int32, (MAIN + EXTRA, 34), 1)
    lead = jnp.logical_and(row < MAIN, row == col)
    rest = jnp.logical_and(col >= MAIN, row - 2 * z == col)
    pick = jnp.where(jnp.logical_or(lead, rest), 1.0, 0.0).astype(bf16)
    own = dot_nt(pick, w1_ref[t]).astype(bf16)
    wa[gid, z] = own[:MAIN]
    exa[z] = own[MAIN:]
    own = dot_nn(pick, w2_ref[t]).astype(bf16)
    wb[gid, z] = own[:MAIN]
    exb[z] = own[MAIN:]
    pl.semaphore_wait(barrier, jnp.where(role == 0, 20, 21))

    pending = []

    def send(ref, at, send_sem, recv_sem, target):
        copy = pltpu.make_async_remote_copy(
            src_ref=ref.at[at], dst_ref=ref.at[at], send_sem=send_sem, recv_sem=recv_sem,
            device_id=target, device_id_type=MESH,
        )
        copy.start()
        pending.append(copy)

    def arrived(ref, at, recv_sem):
        pltpu.make_async_remote_copy(
            src_ref=ref.at[at], dst_ref=ref.at[at], send_sem=recv_sem, recv_sem=recv_sem,
            device_id=partner, device_id_type=MESH,
        ).wait_recv()

    mats = ((wa, ea, exa), (wb, eb, exb))
    z_order = (0, 1, 7, 2, 6, 3, 5, 4)
    y_order = (0, 1, 3, 2)

    def zid(d):
        return lax.rem(z + d, N_Z)

    def gid_of(dy, other=0):
        half = 1 - x_lo if other else x_lo
        return half * N_Y + lax.rem(y + dy, N_Y)

    def send_z(m):
        w, e, ex = mats[m]
        for d in z_order[1:]:
            send(w, (gid, z), send_zm.at[m, d - 1], recv_main.at[m, gid, z], ring_z(d))
            send(ex, z, send_ze.at[m, d - 1], recv_ex.at[m, z], ring_z(d))

    def send_x(m, dy, d):
        w = mats[m][0]
        g, zz = gid_of(dy), zid(d)
        send(w, (g, zz), send_xm.at[m, dy, d], recv_main.at[m, g, zz], partner)

    def send_y(m, d):
        w = mats[m][0]
        zz = zid(d)
        for dy in (1, 3, 2):
            send(w, (gid, zz), send_ym.at[m, dy - 1, d], recv_main.at[m, gid, zz], ring_y(dy))

    def take(m, dy, other, d):
        g, zz = gid_of(dy, other), zid(d)
        arrived(mats[m][0], (g, zz), recv_main.at[m, g, zz])

    def extras(m):
        w, e, ex = mats[m]
        for d in range(1, N_Z):
            arrived(ex, zid(d), recv_ex.at[m, zid(d)])
        total = ex[0].astype(f32)
        for k in range(1, N_Z):
            total += ex[k].astype(f32)
        e[gid] = total.astype(bf16)
        for dy in (1, 3, 2):
            send(e, gid, send_ye.at[m, dy - 1], recv_e.at[m, gid], ring_y(dy))
        send(e, gid, send_xe.at[m, 0], recv_e.at[m, gid], partner)

    def extras_x(m, dy):
        w, e, ex = mats[m]
        g = gid_of(dy)
        arrived(e, g, recv_e.at[m, g])
        send(e, g, send_xe.at[m, dy], recv_e.at[m, g], partner)

    gain = gain_ref[pl.ds(t, 1), :]

    def norm_block(j):
        standard, _ = normalise(x_ref[pl.ds(j * SEG, SEG), :])
        normed[pl.ds(j * SEG, SEG), :] = (standard * gain).astype(bf16)

    def activate(width, weights, slope_at, pool_at):
        pre[:, :width] = dot_nt(normed[...], weights)

        def step(k, carry):
            rows = pl.ds(k * SEG, SEG)
            p = pre[rows, :width]
            u = p * p
            h = 0.5 + 0.5 * jnp.tanh(p * (gelu_c + gelu_k * u))
            value = p * h
            hidden[rows, :width] = value.astype(bf16)
            s = h + value * ((1.0 - h) * (2.0 * gelu_c + 6.0 * gelu_k * u))
            slope_at(rows, s * rowmask_ref[rows, :])
            return carry

        lax.fori_loop(0, ROWS // SEG, step, 0)
        pool_at(dot_nn(pmask_ref[...], hidden[:, :width]))

    hidden = gpre

    def group_forward(g):
        def slope_at(rows, s):
            slope[g, rows, :] = s

        def pool_at(v):
            pooled[g] = v

        activate(GROUP, wa[g].reshape(GROUP, D), slope_at, pool_at)

    def pair(v):
        hi = v.astype(bf16)
        lo = (v - hi.astype(f32)).astype(bf16)
        return jnp.concatenate([hi, lo], axis=0)

    def group_out(g):
        acc[...] += dot_nn(pair(pooled[g]), wb[g].reshape(GROUP, D))

    send_z(0)
    send_y(0, 0)
    send_x(0, 0, 0)
    norm_block(0)
    for k, d in enumerate(z_order[1:]):
        norm_block(k + 1)
        take(0, 0, 0, d)
        send_y(0, d)
        send_x(0, 0, d)
    extras(0)
    send_z(1)
    group_forward(gid)
    for dy in y_order[1:]:
        for d in z_order:
            take(0, dy, 0, d)
            send_x(0, dy, d)
        extras_x(0, dy)
        group_forward(gid_of(dy))

    send_y(1, 0)
    send_x(1, 0, 0)
    for d in z_order[1:]:
        take(1, 0, 0, d)
        send_y(1, d)
        send_x(1, 0, d)
    extras(1)
    for dy in y_order:
        for d in z_order:
            take(0, dy, 1, d)
        arrived(ea, gid_of(dy, 1), recv_e.at[0, gid_of(dy, 1)])
        group_forward(gid_of(dy, 1))

    def slope_at_e(rows, s):
        slope_e[rows, :] = s

    def pool_at_e(v):
        pooled_e[...] = v

    activate(LANES, ea[...].reshape(LANES, D), slope_at_e, pool_at_e)
    sums = dot_nn(pmask_ref[...], x_ref[...])
    acc[...] = jnp.zeros_like(acc)
    group_out(gid)
    for dy in y_order[1:]:
        for d in z_order:
            take(1, dy, 0, d)
            send_x(1, dy, d)
        extras_x(1, dy)
        group_out(gid_of(dy))
    for dy in y_order:
        for d in z_order:
            take(1, dy, 1, d)
        arrived(eb, gid_of(dy, 1), recv_e.at[1, gid_of(dy, 1)])
        group_out(gid_of(dy, 1))
    acc[...] += dot_nn(pair(pooled_e[...]), eb[...].reshape(LANES, D))
    sums = sums + acc[0:8, :] + acc[8:16, :]

    seg = lax.broadcasted_iota(jnp.int32, (8, D), 0)
    first = jnp.sum(sums[0:4], axis=0, keepdims=True)
    second = jnp.sum(sums[4:8], axis=0, keepdims=True)
    sums = jnp.where(is_text, sums, jnp.where(seg < 4, first, second))
    count = count_ref[...]
    value = sums / count
    norm = jnp.sqrt(jnp.sum(value * value, axis=-1, keepdims=True) + norm_eps)
    unit = value / norm

    at16 = lax.broadcasted_iota(jnp.int32, (16, D), 0)
    lead_row = x_lo * 6 + tower * 2
    zero8 = jnp.zeros((8, D), f32)
    low = jnp.where(x_lo == 0, unit, zero8)
    high = jnp.where(x_lo == 0, zero8, unit)
    text_tile = jnp.concatenate([low, high], axis=0)
    image_tile = jnp.where(at16 == lead_row, unit[0:1], jnp.where(at16 == lead_row + 1, unit[4:5], 0.0))
    tile[:, :D] = jnp.where(is_text, text_tile, image_tile).astype(bf16)
    tile[:, D:] = key_ref[...]
    for d in range(1, 8):
        copy = pltpu.make_async_remote_copy(
            src_ref=tile, dst_ref=column.at[role], send_sem=c_send.at[d - 1], recv_sem=c_recv.at[role],
            device_id=in_column(d), device_id_type=MESH,
        )
        copy.start()
        pending.append(copy)
    column[role] = tile[...]
    for d in range(1, 8):
        q = lax.rem(role + d, 8)
        arrived(column, q, c_recv.at[q])
    bundle[0:16, :] = column[5] + column[7]
    images = column[0]
    for q in (1, 2, 3, 4, 6):
        images = images + column[q]
    bundle[16:32, :] = images

    for d in range(1, N_Y):
        copy = pltpu.make_async_remote_copy(
            src_ref=bundle, dst_ref=others.at[d], send_sem=o_send.at[d], recv_sem=o_recv.at[d],
            device_id=device_of(x, y + d, z - role, core), device_id_type=MESH,
        )
        copy.start()
        pending.append(copy)

    def straight():
        return pltpu.make_async_remote_copy(
            src_ref=bundle, dst_ref=others.at[0], send_sem=o_send.at[0], recv_sem=o_recv.at[0],
            device_id=device_of(x, y, z - role, core), device_id_type=MESH,
        )

    @pl.when(role != 0)
    def _():
        copy = straight()
        copy.start()
        copy.wait()

    @pl.when(role == 0)
    def _():
        others[0] = bundle[...]

    for d in range(1, N_Y):
        arrived(others, d, o_recv.at[d])

    scale = scale_ref[0]
    bias = bias_ref[0]
    far = others[...].reshape(N_Y * 32, KEYED)
    logits = scale * dot_nt(bundle[:, :D], far[:, :D]) + bias
    lane = lax.broadcasted_iota(jnp.int32, (32, LANES), 1)
    place = lax.broadcasted_iota(jnp.int32, (32, LANES), 0)
    base = jnp.where(lane == 0, 16.0, jnp.where(lane == 1, 1.0, 0.0)).astype(bf16)
    key_col = dot_nt(base, far[:, D:])
    key_row = dot_nt(bundle[:, D:], jnp.concatenate([base] * 4, axis=0))
    lane32 = lax.rem(lane, 32)
    row_text, col_text = place < 16, lane32 < 16
    row_image = jnp.logical_and(place >= 16, place < 28)
    col_image = jnp.logical_and(lane32 >= 16, lane32 < 28)
    cross = jnp.logical_or(
        jnp.logical_and(row_text, col_image), jnp.logical_and(row_image, col_text)
    )
    match = jnp.where(key_col == key_row, 1.0, 0.0)
    coef = jnp.where(cross, loss_scale * (jax.nn.sigmoid(logits) - match), 0.0).astype(bf16)
    part[...] = (scale * dot_nn(coef, far[:, :D])).reshape(4, 8, D)

    def rows_of(q):
        qx = q // 2
        qlo = lax.rem(qx, 2)
        group = (qx // 2) * 2 + lax.rem(q, 2)
        return jnp.where(group == 3, qlo, 2 + (qlo * 6 + group * 2) // 8)

    for d in range(1, 8):
        q = lax.rem(role + d, 8)
        copy = pltpu.make_async_remote_copy(
            src_ref=part.at[rows_of(q)], dst_ref=gsum.at[role], send_sem=g_send.at[d - 1],
            recv_sem=g_recv.at[role], device_id=in_column(d), device_id_type=MESH,
        )
        copy.start()
        pending.append(copy)
    gsum[role] = part[rows_of(role)]
    for d in range(1, 8):
        q = lax.rem(role + d, 8)
        arrived(gsum, q, g_recv.at[q])
    grad = gsum[0]
    for q in range(1, 8):
        grad = grad + gsum[q]
    mine = lax.rem(lead_row, 8)
    g0 = jnp.sum(jnp.where(seg == mine, grad, 0.0), axis=0, keepdims=True)
    g1 = jnp.sum(jnp.where(seg == mine + 1, grad, 0.0), axis=0, keepdims=True)
    grad = jnp.where(is_text, grad, jnp.where(seg < 4, g0, g1))
    grad = (grad - unit * jnp.sum(unit * grad, axis=-1, keepdims=True)) / norm
    grad = grad / count
    grad_rows = grad.astype(bf16)

    def back(width, weights, slope_of, at):
        gh = dot_nt(grad_rows, weights)
        for j in range(8):
            rows = slice(j * SEG, (j + 1) * SEG)
            gpre[rows, at : at + width] = (slope_of(rows) * gh[j : j + 1, :]).astype(bf16)

    for g in range(8):
        back(GROUP, wb[g].reshape(GROUP, D), lambda rows, g=g: slope[g, rows, :], g * GROUP)
    back(LANES, eb[...].reshape(LANES, D), lambda rows: slope_e[rows, :], 8 * GROUP)
    out_ref[...] = dot_nn(gpre[:, : 8 * GROUP], wa[...].reshape(8 * GROUP, D)) + dot_nn(
        gpre[:, 8 * GROUP :], ea[...].reshape(LANES, D)
    )
    for j in range(8):
        rows = slice(j * SEG, (j + 1) * SEG)
        standard, inv_std = normalise(x_ref[rows, :])
        grad_std = out_ref[rows, :] * gain
        m1 = jnp.mean(grad_std, axis=-1, keepdims=True)
        m2 = jnp.mean(grad_std * standard, axis=-1, keepdims=True)
        out_ref[rows, :] = grad[j : j + 1, :] * rowmask_ref[rows, :] + inv_std * (
            grad_std - m1 - standard * m2
        )
    for copy in pending:
        copy.wait_send()


def body(layer_input, caption_ids, positives, ln_gain, w_first, w_second, logit_scale, logit_bias):
    tower = lax.axis_index("tower")
    blk = lax.axis_index("blk")
    x_lo = blk // (N_Y * N_Z)
    is_text = tower == 3
    mask = jnp.where(is_text, caption_ids != 0, True)
    rowmask = mask.astype(f32).reshape(ROWS, 1)
    same = jnp.arange(ROWS)[None, :] // SEG == jnp.arange(8)[:, None]
    pmask = jnp.where(same, mask.reshape(1, ROWS), False).astype(bf16)
    count = jnp.where(is_text, jnp.sum(mask.astype(f32), axis=1, keepdims=True), 256.0)
    r = jnp.arange(16)
    text_key = 8 * blk + r - 8 * x_lo
    rel = r - (x_lo * 6 + tower * 2)
    two = lax.dynamic_slice_in_dim(positives, 2 * jnp.minimum(tower, 2), 2, 0)
    image_key = jnp.where(rel == 0, two[0], two[1])
    in_text = jnp.logical_and(r >= 8 * x_lo, r < 8 * x_lo + 8)
    in_image = jnp.logical_and(rel >= 0, rel < 2)
    key = jnp.where(is_text, jnp.where(in_text, text_key, 0), jnp.where(in_image, image_key, 0))
    lane = jnp.arange(LANES)[None, :]
    key_tile = jnp.where(lane == 0, (key // 16)[:, None], jnp.where(lane == 1, (key % 16)[:, None], 0))
    key_tile = key_tile.astype(f32).astype(bf16)

    vmem = pl.BlockSpec(memory_space=pltpu.VMEM)
    smem = pl.BlockSpec(memory_space=pltpu.SMEM)
    dma = pltpu.SemaphoreType.DMA
    return pl.pallas_call(
        kernel,
        out_shape=jax.ShapeDtypeStruct((ROWS, D), f32),
        in_specs=[vmem] * 8 + [smem] * 2,
        out_specs=vmem,
        scratch_shapes=[
            pltpu.VMEM((8, N_Z, MAIN, D), bf16),
            pltpu.VMEM((8, N_Z, MAIN, D), bf16),
            pltpu.VMEM((8, EXTRA, D), bf16),
            pltpu.VMEM((8, EXTRA, D), bf16),
            pltpu.VMEM((N_Z, EXTRA, D), bf16),
            pltpu.VMEM((N_Z, EXTRA, D), bf16),
            pltpu.VMEM((ROWS, D), bf16),
            pltpu.VMEM((ROWS, GROUP), f32),
            pltpu.VMEM((8, ROWS, GROUP), f32),
            pltpu.VMEM((ROWS, LANES), f32),
            pltpu.VMEM((8, 8, GROUP), f32),
            pltpu.VMEM((8, LANES), f32),
            pltpu.VMEM((16, D), f32),
            pltpu.VMEM((16, KEYED), bf16),
            pltpu.VMEM((8, 16, KEYED), bf16),
            pltpu.VMEM((32, KEYED), bf16),
            pltpu.VMEM((N_Y, 32, KEYED), bf16),
            pltpu.VMEM((4, 8, D), f32),
            pltpu.VMEM((8, 8, D), f32),
            pltpu.VMEM((ROWS, 8 * GROUP + LANES), bf16),
            dma((2, 8, 8)),
            dma((2, 8)),
            dma((2, 8)),
            dma((2, 7)),
            dma((2, 7)),
            dma((2, 3, 8)),
            dma((2, 3)),
            dma((2, 4, 8)),
            dma((2, 4)),
            dma((7,)),
            dma((8,)),
            dma((4,)),
            dma((4,)),
            dma((7,)),
            dma((8,)),
        ],
        compiler_params=pltpu.CompilerParams(
            collective_id=0, has_side_effects=True, vmem_limit_bytes=56 * 2**20
        ),
        name="step",
    )(
        layer_input, rowmask, pmask, count, key_tile, ln_gain, w_first, w_second,
        logit_scale, logit_bias,
    )


def solution(mesh):
    placed = (
        P(("blk", "tower"), None),
        P("blk", None),
        P("blk"),
        P(),
        P(None, None, "blk"),
        P(None, "blk", None),
        P(),
        P(),
    )
    return jax.shard_map(
        body, mesh=mesh, in_specs=placed, out_specs=P(("blk", "tower"), None), check_vma=False
    )
```

time: 1350 us -> 148 us (0.11)
  waiting for transfers between devices: 812 us -> 0 us
  blocking collectives: 444 us -> 0 us
  Pallas kernels: 0 us -> 133 us
  matrix products: 36.1 us -> 0 us
  local copies, waits for them, and re-layouts: 27.2 us -> 9.86 us
  between operations: 15.2 us -> 1.33 us
    all_gather x3 -> x0, waiting for transfers between devices: 812 us -> none  [the longest x1 287 us: body(): lax.all_gather(second, 'blk', axis=0, tiled=True)]
    unnamed x1 -> x0, blocking collectives: 279 us -> none
    psum x2 -> x0, blocking collectives: 164 us -> none  [the longest x1 111 us: body(): lax.psum(span_grad.astype(jnp.bfloat16), 'tower').astype(jnp.float32)]
    pallas_call x0 -> x1, Pallas kernels: none -> 133 us  [body(): pl.pallas_call(kernel, out_shape=jax.ShapeDtypeStruct((ROWS, D), f32), in...]
    dot_general x6 -> x0, matrix products: 36.1 us -> none  [the longest x2 16.4 us: contract_last(): lax.dot_general(left, right, (((1,), (1,)), ((), ())), preferred_element_...]
    all_gather x1 -> x0, local copies, waits for them, and re-layouts: 22.1 us -> none  [body(): lax.all_gather(first, 'blk', axis=1, tiled=True)]
  transfers between devices with their start and end apart: 3 -> 0, of which waited for: 3 -> 0; matrix products, arithmetic and copies ran while one was open for 3% -> 0% of each run, Pallas kernels for 0% -> 0%
where the time goes in v1:
time: 148 us; the launch traced here: 147 us
  Pallas kernels  133 us (90%)
  local copies, waits for them, and re-layouts  9.86 us (7%)
  other arithmetic  3.39 us (2%)
    pallas_call x1, Pallas kernels, body(): pl.pallas_call(kernel, out_shape=jax.ShapeDtypeStruct((ROWS, D), f32), in...  133 us
    unnamed x3, local copies, waits for them, and re-layouts  6.85 us

profile of v1, /device:TPU:1, one launch (start us, length us, event | category | flops | bytes accessed | tf_op | source)
XLA Modules:
  0.0 147.3 jit_solution(16380307658018805101)
XLA Ops:
  1.3 0.7 dynamic_slice.3
  2.0 0.6 fusion.6
  2.6 1.3 and_select_fusion.1
  4.0 0.8 convert_reduce_fusion
  4.8 0.1 broadcast_in_dim.78
  4.9 0.7 convert_convert_fusion.key_ref
  5.5 0.7 copy.13.count_ref
  6.2 0.6 fusion.1.pmask_ref
  6.8 1.6 %copy.15.w2_ref = bf16[2,34,1152]{2,1,0:T(8,128)(2,1)} copy(bf16[2,34,1152]{2,0,1:T(2,128)(2,1)} %param.13) | data formatting | bytes 313344 | tf_op args[5]
  8.4 0.9 reshape.112.rowmask_ref
  9.3 2.0 %copy.14.w1_ref = bf16[2,1152,34]{2,1,0:T(8,128)(2,1)} copy(bf16[2,1152,34]{1,0,2:T(2,128)(2,1)} %param.12) | data formatting | bytes 313344 | tf_op args[4]
  11.4 132.7 %step.1 = f32[512,1152]{1,0:T(8,128)} custom-call(bf16[512,1152]{1,0:T(8,128)(2,1)} %x_ref.1, f32[512,1]{1,0:T(8,128)} %reshape.112.rowmask_ref, bf16[8,512]{1,0:T(8,128)(2,1)} %fusion.1.pmask_ref, f32[8,1]{1,0:T(8,128)} %copy.13.count_ref, bf16[16,128]{1,0:T(8,128)(2,1)} %convert_convert_fusion.key_ref, f32[2,1152]{1,0:T(2,128)} %gain_ref.1, ...), custom_call_target="tpu_custom_call" | custom-call | tf_op jit(solution)/shard_map/step/pallas_call | solution.py:440
  144.0 3.2 %copy.19 = f32[512,1152]{1,0:T(8,128)} copy(f32[512,1152]{1,0:T(8,128)} %step.1) | data formatting | bytes 4718592
  (5 shorter events, 0.0 us)

commit v2 on v1

v2 whole, which is shorter than its diff:
```python
import functools

import jax
import jax.numpy as jnp
from jax import lax
from jax.experimental import pallas as pl
from jax.experimental.pallas import tpu as pltpu
from jax.sharding import PartitionSpec as P

D = 1152
ROWS = 512
N_Y = 4
N_Z = 8
MAIN = 32
GROUP = N_Z * MAIN
EXTRA = 16
SEG = 64
LANES = 128
KEYED = D + LANES
FRONT = 896
SECOND = 14.0

norm_eps = 1e-06
loss_scale = 128.0
gelu_c = 0.7978845608028654
gelu_k = gelu_c * 0.044715

MESH = pl.DeviceIdType.MESH
bf16 = jnp.bfloat16
f32 = jnp.float32


def dot_nt(left, right):
    return lax.dot_general(left, right, (((1,), (1,)), ((), ())), preferred_element_type=f32)


def dot_nn(left, right):
    return jnp.dot(left, right, preferred_element_type=f32)


def device_of(x, y, z, core):
    x = lax.rem(x + 8, 4)
    y = lax.rem(y + 8, N_Y)
    z = lax.rem(z + 16, N_Z)
    return (lax.rem(x, 2) * (N_Y * N_Z) + y * N_Z + z, (x // 2) * 2 + core)


def normalise(rows):
    values = rows.astype(f32)
    centered = values - jnp.mean(values, axis=-1, keepdims=True)
    variance = jnp.mean(centered * centered, axis=-1, keepdims=True)
    inv_std = lax.rsqrt(variance + norm_eps)
    return centered * inv_std, inv_std


def kernel(
    x_ref, ids_ref, gain_ref, w1_ref, w2_ref, positive_ref, scale_ref, bias_ref,
    out_ref,
    wa, wb, ea, eb, exa, exb, normed, pre, slope, slope_e, pooled, pooled_e, acc,
    pmask, rowmask, tile_t, tile_i, column_t, column_i, bundle, others,
    part_t, part_i, gsum_t, gsum_i, grad_at, gpre,
    recv_main, recv_by, recv_bx, recv_bz, send_by, send_bx, send_bl, send_bs, recv_ex, recv_e, send_zm, send_ze, send_ym, send_ye, send_xm, send_xe,
    c_send, c_recv, o_send, o_recv, g_send, g_recv,
):
    blk = lax.axis_index("blk")
    tower = lax.axis_index("tower")
    x_lo = blk // (N_Y * N_Z)
    y = lax.rem(blk // N_Z, N_Y)
    z = lax.rem(blk, N_Z)
    x_hi = tower // 2
    core = lax.rem(tower, 2)
    x = x_hi * 2 + x_lo
    is_text = tower == 3
    t = jnp.where(is_text, 1, 0)
    role = x * 2 + core
    gid = x_lo * N_Y + y

    def far_at(k):
        side = 1 - 2 * core
        odd = lax.rem(x, 2)
        dy = jnp.where(odd == 1, 2 * (k // 2) + x // 2, k)
        dz = jnp.where(odd == 1, side * (1 + 2 * (k % 2)), jnp.where(x == 0, 4 * core, 2 * side))
        return dy, dz

    def far_from(k):
        dy, dz = far_at(k)
        return device_of(x, y - dy, z + dz, core)

    def far_to(k):
        dy, dz = far_at(k)
        return device_of(x, y + dy, z - dz, core)

    toward = jnp.where(core == 1, 1 - 2 * x_lo, 2 * x_lo - 1)
    partner = device_of(x + toward, y, z, core)

    def ring_z(d):
        return device_of(x, y, z + d, core)

    def ring_y(d):
        return device_of(x, y + d, z, core)

    def in_column(d):
        q = lax.rem(role + d, 8)
        return device_of(q // 2, y, z, lax.rem(q, 2))

    barrier = pltpu.get_barrier_semaphore()
    for d in range(1, N_Z):
        pl.semaphore_signal(barrier, inc=1, device_id=ring_z(d), device_id_type=MESH)
    for d in range(1, N_Y):
        pl.semaphore_signal(barrier, inc=1, device_id=ring_y(d), device_id_type=MESH)
    for d in range(1, 8):
        pl.semaphore_signal(barrier, inc=1, device_id=in_column(d), device_id_type=MESH)
    for k in range(1, N_Y):
        pl.semaphore_signal(barrier, inc=1, device_id=far_from(k), device_id_type=MESH)

    @pl.when(role != 0)
    def _():
        pl.semaphore_signal(barrier, inc=1, device_id=far_from(0), device_id_type=MESH)

    row = lax.broadcasted_iota(jnp.int32, (MAIN + EXTRA, 68), 0)
    col = lax.broadcasted_iota(jnp.int32, (MAIN + EXTRA, 68), 1)
    lead = jnp.logical_and(row < MAIN, 2 * row + t == col)
    rest = jnp.logical_and(col >= 2 * MAIN, 2 * (row - 2 * z) + t == col)
    pick = jnp.where(jnp.logical_or(lead, rest), 1.0, 0.0).astype(bf16)
    for ref, w, ex in ((w1_ref, wa, exa), (w2_ref, wb, exb)):
        own = dot_nn(pick, ref[...].reshape(68, D)).astype(bf16)
        w[gid, z] = own[:MAIN]
        ex[0] = own[MAIN:]

    mask = jnp.where(is_text, jnp.where(ids_ref[...] != 0, 1.0, 0.0), 1.0)
    count = jnp.where(is_text, jnp.sum(mask, axis=1, keepdims=True), 256.0)
    slot = lax.broadcasted_iota(jnp.int32, (SEG, ROWS), 0)
    at = lax.broadcasted_iota(jnp.int32, (SEG, ROWS), 1)
    spread = jnp.where(lax.rem(at, SEG) == slot, 1.0, 0.0).astype(bf16)
    wide = dot_nn(mask.astype(bf16), spread)
    segment = lax.broadcasted_iota(jnp.int32, (8, ROWS), 0)
    at = lax.broadcasted_iota(jnp.int32, (8, ROWS), 1)
    pmask[...] = jnp.where(at // SEG == segment, wide, 0.0).astype(bf16)
    rowmask[...] = lax.dot_general(
        pmask[...], jnp.ones((8, LANES), bf16), (((0,), (0,)), ((), ())), preferred_element_type=f32
    )

    def mask_of(rows, width):
        return jnp.concatenate([rowmask[rows, :]] * (width // LANES), axis=1)

    pl.semaphore_wait(barrier, jnp.where(role == 0, 20, 21))

    pending = []

    def send(ref, at, send_sem, recv_sem, target):
        copy = pltpu.make_async_remote_copy(
            src_ref=ref.at[at], dst_ref=ref.at[at], send_sem=send_sem, recv_sem=recv_sem,
            device_id=target, device_id_type=MESH,
        )
        copy.start()
        pending.append(copy)

    def arrived(ref, at, recv_sem):
        pltpu.make_async_remote_copy(
            src_ref=ref.at[at], dst_ref=ref.at[at], send_sem=recv_sem, recv_sem=recv_sem,
            device_id=partner, device_id_type=MESH,
        ).wait_recv()

    mats = ((wa, ea, exa), (wb, eb, exb))
    z_order = (0, 1, 7, 2, 6, 3, 5, 4)
    y_order = (0, 1, 3, 2)

    def zid(d):
        return lax.rem(z + d, N_Z)

    def gid_of(dy, other=0):
        half = 1 - x_lo if other else x_lo
        return half * N_Y + lax.rem(y + dy, N_Y)

    front = pl.ds(0, FRONT)
    back_cols = pl.ds(FRONT, D - FRONT)
    every = pl.ds(0, MAIN)
    long = 1 - 2 * core

    def half_of(other):
        return pl.ds((1 - x_lo if other else x_lo) * N_Y, N_Y)

    def send_z(m):
        for d in z_order[1:]:
            send(mats[m][0], (gid, z, every, front), send_zm.at[m, d - 1], recv_main.at[m, gid, z], ring_z(d))

    def send_x(m, dy, d):
        g, zz = gid_of(dy), zid(d)
        send(mats[m][0], (g, zz, every, front), send_xm.at[m, dy, d], recv_main.at[m, g, zz], partner)

    def send_y(m, d):
        zz = zid(d)
        for dy in (1, 3, 2):
            send(
                mats[m][0], (gid, zz, every, front), send_ym.at[m, dy - 1, d], recv_main.at[m, gid, zz], ring_y(dy)
            )

    def take(m, dy, other, d):
        g, zz = gid_of(dy, other), zid(d)
        arrived(mats[m][0], (g, zz, every, front), recv_main.at[m, g, zz])

    def back_y(m):
        for dy in (1, 3, 2):
            send(mats[m][0], (gid, z, every, back_cols), send_by.at[m, dy - 1], recv_by.at[m, y], ring_y(dy))

    def back_ring(m, other, hop):
        at = lambda zz: (half_of(other), zz, every, back_cols)
        h = 1 if other else 0
        w = mats[m][0]
        there = lax.rem(z - long * hop + 2 * N_Z, N_Z)
        here = lax.rem(z + long * hop + 2 * N_Z, N_Z)
        half = 1 - x_lo if other else x_lo
        if 0 < hop:
            arrived(w, at(there), recv_bz.at[m, half, there])
            if hop < 4:
                arrived(w, at(here), recv_bz.at[m, half, here])
        if hop < 4:
            send(w, at(there), send_bl.at[m, h, hop], recv_bz.at[m, half, there], ring_z(long))
        if hop < 3:
            send(w, at(here), send_bs.at[m, h, hop], recv_bz.at[m, half, here], ring_z(-long))

    def back_own(m):
        w = mats[m][0]
        for dy in (1, 3, 2):
            yy = lax.rem(y + dy, N_Y)
            arrived(w, (gid_of(dy), z, every, back_cols), recv_by.at[m, yy])
        send(w, (half_of(0), z, every, back_cols), send_bx.at[m], recv_bx.at[m], partner)
        back_ring(m, 0, 0)

    def back_partner(m):
        arrived(mats[m][0], (half_of(1), z, every, back_cols), recv_bx.at[m])
        back_ring(m, 1, 0)

    def extras_send(m, k):
        w, e, ex = mats[m]
        bit = 1 << k
        other = z + bit - 2 * bit * lax.rem(z // bit, 2)
        copy = pltpu.make_async_remote_copy(
            src_ref=ex.at[2 * k], dst_ref=ex.at[2 * k + 1], send_sem=send_ze.at[m, k],
            recv_sem=recv_ex.at[m, k], device_id=device_of(x, y, other, core), device_id_type=MESH,
        )
        copy.start()
        pending.append(copy)

    def extras_take(m, k):
        w, e, ex = mats[m]
        arrived(ex, 2 * k + 1, recv_ex.at[m, k])
        total = (ex[2 * k].astype(f32) + ex[2 * k + 1].astype(f32)).astype(bf16)
        if k < 2:
            ex[2 * k + 2] = total
            extras_send(m, k + 1)
            return
        e[gid] = total
        for dy in (1, 3, 2):
            send(e, gid, send_ye.at[m, dy - 1], recv_e.at[m, gid], ring_y(dy))
        send(e, gid, send_xe.at[m, 0], recv_e.at[m, gid], partner)

    def extras_x(m, dy):
        w, e, ex = mats[m]
        g = gid_of(dy)
        arrived(e, g, recv_e.at[m, g])
        send(e, g, send_xe.at[m, dy], recv_e.at[m, g], partner)

    gain = gain_ref[pl.ds(t, 1), :]

    def norm_block(j):
        standard, _ = normalise(x_ref[pl.ds(j * SEG, SEG), :])
        normed[pl.ds(j * SEG, SEG), :] = (standard * gain).astype(bf16)

    def activate(width, weights, slope_at, pool_at):
        pre[:, :width] = dot_nt(normed[...], weights)

        def step(k, carry):
            rows = pl.ds(k * SEG, SEG)
            p = pre[rows, :width]
            u = p * p
            h = 0.5 + 0.5 * jnp.tanh(p * (gelu_c + gelu_k * u))
            value = p * h
            hidden[rows, :width] = value.astype(bf16)
            s = h + value * ((1.0 - h) * (2.0 * gelu_c + 6.0 * gelu_k * u))
            slope_at(rows, s * mask_of(rows, width))
            return carry

        lax.fori_loop(0, ROWS // SEG, step, 0)
        pool_at(dot_nn(pmask[...], hidden[:, :width]))

    hidden = gpre

    def group_forward(g):
        def slope_at(rows, s):
            slope[g, rows, :] = s

        def pool_at(v):
            pooled[g] = v

        activate(GROUP, wa[g].reshape(GROUP, D), slope_at, pool_at)

    def pair(v):
        hi = v.astype(bf16)
        lo = (v - hi.astype(f32)).astype(bf16)
        return jnp.concatenate([hi, lo], axis=0)

    def group_out(g):
        acc[...] += dot_nn(pair(pooled[g]), wb[g].reshape(GROUP, D))

    def slope_at_e(rows, s):
        slope_e[rows, :] = s

    def pool_at_e(v):
        pooled_e[...] = v

    steps = []

    def due(when, act, *args):
        steps.append((when, len(steps), act, args))

    def start(m):
        send_z(m)
        back_y(m)
        send_y(m, 0)
        send_x(m, 0, 0)
        extras_send(m, 0)

    def z_arrival(m, d):
        take(m, 0, 0, d)
        send_y(m, d)
        send_x(m, 0, d)

    def y_arrival(m, d):
        for dy in y_order[1:]:
            take(m, dy, 0, d)
            send_x(m, dy, d)

    def x_arrival(m, dy):
        for d in z_order:
            take(m, dy, 1, d)

    def extras_rest(m):
        for dy in y_order[1:]:
            extras_x(m, dy)

    def extras_last(m):
        for dy in y_order:
            arrived(mats[m][1], gid_of(dy, 1), recv_e.at[m, gid_of(dy, 1)])

    for j in range(8):
        due(0.1 + 1.0 * j, norm_block, j)
    for m, at in ((0, 0.0), (1, SECOND)):
        due(at, start, m)
        for n, d in enumerate(z_order[1:]):
            due(at + 4.4 + 1.3 * n, z_arrival, m, d)
        for n, d in enumerate(z_order):
            due(at + 7.0 + 2.3 * n, y_arrival, m, d)
        due(at + 5.0, back_own, m)
        due(at + 8.0, back_partner, m)
        for hop in range(1, 5):
            due(at + 6.0 + 4.0 * hop, back_ring, m, 0, hop)
            due(at + 9.0 + 4.0 * hop, back_ring, m, 1, hop)
        due(at + 6.5, extras_take, m, 0)
        due(at + 10.5, extras_take, m, 1)
        due(at + 15.5, extras_take, m, 2)
        due(at + 24.2, extras_rest, m)
        due(at + 26.0, extras_last, m)
    for n, dy in enumerate(y_order):
        due(25.1 + 1.4 * n, group_forward, gid_of(dy))
        due(30.6 + 1.4 * n, x_arrival, 0, dy)
        due(30.7 + 1.4 * n, group_forward, gid_of(dy, 1))

    def forward_e():
        activate(LANES, ea[...].reshape(LANES, D), slope_at_e, pool_at_e)

    due(36.5, forward_e)
    for act in sorted(steps):
        act[2](*act[3])
    sums = dot_nn(pmask[...], x_ref[...])
    acc[...] = jnp.zeros_like(acc)
    for dy in y_order:
        group_out(gid_of(dy))
    for dy in y_order:
        x_arrival(1, dy)
        group_out(gid_of(dy, 1))
    acc[...] += dot_nn(pair(pooled_e[...]), eb[...].reshape(LANES, D))
    sums = sums + acc[0:8, :] + acc[8:16, :]

    seg = lax.broadcasted_iota(jnp.int32, (8, D), 0)
    first = jnp.sum(sums[0:4], axis=0, keepdims=True)
    second = jnp.sum(sums[4:8], axis=0, keepdims=True)
    sums = jnp.where(is_text, sums, jnp.where(seg < 4, first, second))
    value = sums / count
    norm = jnp.sqrt(jnp.sum(value * value, axis=-1, keepdims=True) + norm_eps)
    unit = value / norm

    key_at = lax.broadcasted_iota(jnp.int32, (8, LANES), 0)
    key_lane = lax.broadcasted_iota(jnp.int32, (8, LANES), 1)
    group = jnp.minimum(tower, 2)
    image_key = jnp.where(key_at == 0, positive_ref[2 * group], positive_ref[2 * group + 1])
    key = jnp.where(is_text, 8 * blk + key_at, image_key)
    key = jnp.where(key_lane == 0, key >> 4, jnp.where(key_lane == 1, key & 15, 0)).astype(f32)
    keyed = jnp.concatenate([unit, key], axis=1)
    half = KEYED // 2
    tile_t[...] = jnp.concatenate([keyed[:, :half], keyed[:, half:]], axis=0).astype(bf16)
    two = jnp.concatenate([jnp.concatenate([unit[0:1], unit[4:5]], axis=0), key[0:2]], axis=1)
    fifth = KEYED // 5
    parts = [two[:, p * fifth : (p + 1) * fifth] for p in range(5)]
    tile_i[...] = jnp.concatenate(parts + [jnp.zeros((6, fifth), f32)], axis=0).astype(bf16)

    def to_column(text, d):
        if text:
            src, dst = tile_t, column_t.at[x_lo]
        else:
            src, dst = tile_i, column_i.at[x_lo * 3 + tower]
        return pltpu.make_async_remote_copy(
            src_ref=src, dst_ref=dst, send_sem=c_send.at[d - 1], recv_sem=c_recv.at[role],
            device_id=in_column(d), device_id_type=MESH,
        )

    @pl.when(is_text)
    def _():
        for d in range(1, 8):
            to_column(True, d).start()
        column_t[x_lo] = tile_t[...]

    @pl.when(jnp.logical_not(is_text))
    def _():
        for d in range(1, 8):
            to_column(False, d).start()
        column_i[x_lo * 3 + tower] = tile_i[...]

    def place_of(q):
        qx, qc = q // 2, q % 2
        g = (qx // 2) * 2 + qc
        return g == 3, qx % 2 if g == 3 else (qx % 2) * 3 + g

    for q in range(8):
        text, place = place_of(q)

        @pl.when(role != q)
        def _():
            arrived(column_t if text else column_i, place, c_recv.at[q])

    rows = []
    for k in range(2):
        v = column_t[k].astype(f32)
        rows.append(jnp.concatenate([v[0:8], v[8:16]], axis=1))
    bundle[0:16, :] = jnp.concatenate(rows, axis=0).astype(bf16)
    rows = []
    for k in range(6):
        v = column_i[k].astype(f32)
        rows.append(jnp.concatenate([v[2 * p : 2 * p + 2] for p in range(5)], axis=1))
    rows.append(jnp.zeros((4, KEYED), f32))
    bundle[16:32, :] = jnp.concatenate(rows, axis=0).astype(bf16)

    for d in range(1, N_Y):
        copy = pltpu.make_async_remote_copy(
            src_ref=bundle, dst_ref=others.at[d], send_sem=o_send.at[d], recv_sem=o_recv.at[d],
            device_id=far_to(d), device_id_type=MESH,
        )
        copy.start()
        pending.append(copy)

    def straight():
        return pltpu.make_async_remote_copy(
            src_ref=bundle, dst_ref=others.at[0], send_sem=o_send.at[0], recv_sem=o_recv.at[0],
            device_id=far_to(0), device_id_type=MESH,
        )

    @pl.when(role != 0)
    def _():
        copy = straight()
        copy.start()
        copy.wait()

    @pl.when(role == 0)
    def _():
        others[0] = bundle[...]

    for d in range(1, N_Y):
        arrived(others, d, o_recv.at[d])

    scale = scale_ref[0]
    bias = bias_ref[0]
    far = others[...].reshape(N_Y * 32, KEYED)
    logits = scale * dot_nt(bundle[:, :D], far[:, :D]) + bias
    lane = lax.broadcasted_iota(jnp.int32, (32, LANES), 1)
    place = lax.broadcasted_iota(jnp.int32, (32, LANES), 0)
    base = jnp.where(lane == 0, 16.0, jnp.where(lane == 1, 1.0, 0.0)).astype(bf16)
    key_col = dot_nt(base, far[:, D:])
    key_row = dot_nt(bundle[:, D:], jnp.concatenate([base] * 4, axis=0))
    lane32 = lax.rem(lane, 32)
    row_text, col_text = place < 16, lane32 < 16
    row_image = jnp.logical_and(place >= 16, place < 28)
    col_image = jnp.logical_and(lane32 >= 16, lane32 < 28)
    cross = jnp.logical_or(
        jnp.logical_and(row_text, col_image), jnp.logical_and(row_image, col_text)
    )
    match = jnp.where(key_col == key_row, 1.0, 0.0)
    coef = jnp.where(cross, loss_scale * (jax.nn.sigmoid(logits) - match), 0.0).astype(bf16)
    share = scale * dot_nn(coef, far[:, :D])
    third = D // 3
    for k in range(2):
        part_t[k] = share[8 * k : 8 * k + 8]
    for k in range(6):
        v = share[16 + 2 * k : 18 + 2 * k]
        v = [v[:, p * third : (p + 1) * third] for p in range(3)] + [jnp.zeros((2, third), f32)]
        part_i[k] = jnp.concatenate(v, axis=0)

    def to_owner(q):
        text, place = place_of(q)
        src, dst = (part_t, gsum_t) if text else (part_i, gsum_i)
        return pltpu.make_async_remote_copy(
            src_ref=src.at[place], dst_ref=dst.at[role], send_sem=g_send.at[q], recv_sem=g_recv.at[role],
            device_id=device_of(q // 2, y, z, q % 2), device_id_type=MESH,
        )

    for q in range(8):

        @pl.when(role != q)
        def _():
            to_owner(q).start()

    @pl.when(is_text)
    def _():
        gsum_t[role] = part_t[x_lo]
        for d in range(1, 8):
            q = lax.rem(role + d, 8)
            arrived(gsum_t, q, g_recv.at[q])
        v = gsum_t[0]
        for q in range(1, 8):
            v = v + gsum_t[q]
        grad_at[...] = v

    @pl.when(jnp.logical_not(is_text))
    def _():
        gsum_i[role] = part_i[x_lo * 3 + tower]
        for d in range(1, 8):
            q = lax.rem(role + d, 8)
            arrived(gsum_i, q, g_recv.at[q])
        v = gsum_i[0]
        for q in range(1, 8):
            v = v + gsum_i[q]
        v = jnp.concatenate([v[2 * p : 2 * p + 2] for p in range(3)], axis=1)
        grad_at[...] = jnp.where(seg < 4, v[0:1], v[1:2])

    grad = grad_at[...]
    grad = (grad - unit * jnp.sum(unit * grad, axis=-1, keepdims=True)) / norm
    grad = grad / count
    grad_rows = grad.astype(bf16)

    def back(width, weights, slope_of, at):
        gh = dot_nt(grad_rows, weights)
        for j in range(8):
            rows = slice(j * SEG, (j + 1) * SEG)
            gpre[rows, at : at + width] = (slope_of(rows) * gh[j : j + 1, :]).astype(bf16)

    for g in range(8):
        back(GROUP, wb[g].reshape(GROUP, D), lambda rows, g=g: slope[g, rows, :], g * GROUP)
    back(LANES, eb[...].reshape(LANES, D), lambda rows: slope_e[rows, :], 8 * GROUP)
    out_ref[...] = dot_nn(gpre[:, : 8 * GROUP], wa[...].reshape(8 * GROUP, D)) + dot_nn(
        gpre[:, 8 * GROUP :], ea[...].reshape(LANES, D)
    )
    for j in range(8):
        rows = slice(j * SEG, (j + 1) * SEG)
        standard, inv_std = normalise(x_ref[rows, :])
        grad_std = out_ref[rows, :] * gain
        m1 = jnp.mean(grad_std, axis=-1, keepdims=True)
        m2 = jnp.mean(grad_std * standard, axis=-1, keepdims=True)
        out_ref[rows, :] = grad[j : j + 1, :] * mask_of(rows, D) + inv_std * (
            grad_std - m1 - standard * m2
        )
    for copy in pending:
        copy.wait_send()

    @pl.when(is_text)
    def _():
        for d in range(1, 8):
            to_column(True, d).wait_send()

    @pl.when(jnp.logical_not(is_text))
    def _():
        for d in range(1, 8):
            to_column(False, d).wait_send()

    for q in range(8):

        @pl.when(role != q)
        def _():
            to_owner(q).wait_send()


def body(layer_input, caption_ids, positives, ln_gain, w_first, w_second, logit_scale, logit_bias):
    vmem = pl.BlockSpec(memory_space=pltpu.VMEM)
    smem = pl.BlockSpec(memory_space=pltpu.SMEM)
    dma = pltpu.SemaphoreType.DMA
    return pl.pallas_call(
        kernel,
        out_shape=jax.ShapeDtypeStruct((ROWS, D), f32),
        in_specs=[vmem] * 5 + [smem] * 3,
        out_specs=vmem,
        scratch_shapes=[
            pltpu.VMEM((8, N_Z, MAIN, D), bf16),
            pltpu.VMEM((8, N_Z, MAIN, D), bf16),
            pltpu.VMEM((8, EXTRA, D), bf16),
            pltpu.VMEM((8, EXTRA, D), bf16),
            pltpu.VMEM((6, EXTRA, D), bf16),
            pltpu.VMEM((6, EXTRA, D), bf16),
            pltpu.VMEM((ROWS, D), bf16),
            pltpu.VMEM((ROWS, GROUP), f32),
            pltpu.VMEM((8, ROWS, GROUP), f32),
            pltpu.VMEM((ROWS, LANES), f32),
            pltpu.VMEM((8, 8, GROUP), f32),
            pltpu.VMEM((8, LANES), f32),
            pltpu.VMEM((16, D), f32),
            pltpu.VMEM((8, ROWS), bf16),
            pltpu.VMEM((ROWS, LANES), f32),
            pltpu.VMEM((16, KEYED // 2), bf16),
            pltpu.VMEM((16, KEYED // 5), bf16),
            pltpu.VMEM((2, 16, KEYED // 2), bf16),
            pltpu.VMEM((6, 16, KEYED // 5), bf16),
            pltpu.VMEM((32, KEYED), bf16),
            pltpu.VMEM((N_Y, 32, KEYED), bf16),
            pltpu.VMEM((2, 8, D), f32),
            pltpu.VMEM((6, 8, D // 3), f32),
            pltpu.VMEM((8, 8, D), f32),
            pltpu.VMEM((8, 8, D // 3), f32),
            pltpu.VMEM((8, D), f32),
            pltpu.VMEM((ROWS, 8 * GROUP + LANES), bf16),
            dma((2, 8, 8)),
            dma((2, 4)),
            dma((2,)),
            dma((2, 2, 8)),
            dma((2, 3)),
            dma((2,)),
            dma((2, 2, 4)),
            dma((2, 2, 3)),
            dma((2, 3)),
            dma((2, 8)),
            dma((2, 7)),
            dma((2, 3)),
            dma((2, 3, 8)),
            dma((2, 3)),
            dma((2, 4, 8)),
            dma((2, 4)),
            dma((7,)),
            dma((8,)),
            dma((4,)),
            dma((4,)),
            dma((8,)),
            dma((8,)),
        ],
        compiler_params=pltpu.CompilerParams(
            collective_id=0, has_side_effects=True, vmem_limit_bytes=56 * 2**20
        ),
        name="step",
    )(
        layer_input, caption_ids, ln_gain, jnp.transpose(w_first, (2, 0, 1)), jnp.transpose(w_second, (1, 0, 2)),
        positives, logit_scale, logit_bias,
    )


def solution(mesh):
    placed = (
        P(("blk", "tower"), None),
        P("blk", None),
        P("blk"),
        P(),
        P(None, None, "blk"),
        P(None, "blk", None),
        P(),
        P(),
    )
    return jax.shard_map(
        body, mesh=mesh, in_specs=placed, out_specs=P(("blk", "tower"), None), check_vma=False
    )
```

time: 148 us -> 114 us (0.77)
  Pallas kernels: 133 us -> 109 us
  local copies, waits for them, and re-layouts: 9.86 us -> 3.22 us
  other arithmetic: 3.39 us -> 0 us
    pallas_call x1, Pallas kernels: 133 us -> 109 us  [body(): pl.pallas_call(kernel, out_shape=jax.ShapeDtypeStruct((ROWS, D), f32), in...]
    unnamed x3 -> x1, local copies, waits for them, and re-layouts: 6.85 us -> 3.22 us
where the time goes in v2:
time: 114 us
  Pallas kernels  109 us (96%)
  local copies, waits for them, and re-layouts  3.22 us (3%)
  between operations  1.31 us (1%)
    pallas_call x1, Pallas kernels, body(): pl.pallas_call(kernel, out_shape=jax.ShapeDtypeStruct((ROWS, D), f32), in...  109 us
    unnamed x1, local copies, waits for them, and re-layouts  3.22 us

profile of v2, /device:TPU:1, one launch (start us, length us, event | category | flops | bytes accessed | tf_op | source)
XLA Modules:
  0.0 113.9 jit_solution(10386031867634992723)
XLA Ops:
  1.3 109.3 %step.1 = f32[512,1152]{1,0:T(8,128)} custom-call(bf16[512,1152]{1,0:T(8,128)(2,1)} %x_ref.1, s32[8,64]{1,0:T(8,128)} %ids_ref.1, f32[2,1152]{1,0:T(2,128)} %gain_ref.1, bf16[34,2,1152]{2,1,0:T(2,128)(2,1)} %bitcast.2, bf16[34,2,1152]{2,1,0:T(2,128)(2,1)} %bitcast.3, s32[6]{0:T(128)} %positive_ref.1, f32[1]{0:T(128)S(6)} %copy.10.scale_ref, f32[1]{0:T(128)S(6)} %copy.11.bias_ref), custom_call_target="tpu_custom_call" | custom-call | tf_op jit(solution)/shard_map/step/pallas_call | solution.py:594
  110.6 3.2 %copy.12 = f32[512,1152]{1,0:T(8,128)} copy(f32[512,1152]{1,0:T(8,128)} %step.1) | data formatting | bytes 4718592

commit v3 on v2

--- a/solution.py
+++ b/solution.py
@@ -17,8 +17,8 @@
 SEG = 64
 LANES = 128
 KEYED = D + LANES
-FRONT = 896
-SECOND = 14.0
+FRONT = 768
+SECOND = 22.0
 
 norm_eps = 1e-06
 loss_scale = 128.0
@@ -54,8 +54,9 @@
 
 
 def kernel(
-    x_ref, ids_ref, gain_ref, w1_ref, w2_ref, positive_ref, scale_ref, bias_ref,
-    out_ref,
+    x_hbm, ids_hbm, gain_hbm, w1_hbm, w2_hbm, positive_ref, scale_ref, bias_ref,
+    out_hbm,
+    x_ref, ids_ref, gain_ref, w1_ref, w2_ref, out_ref, in_sem, out_sem,
     wa, wb, ea, eb, exa, exb, normed, pre, slope, slope_e, pooled, pooled_e, acc,
     pmask, rowmask, tile_t, tile_i, column_t, column_i, bundle, others,
     part_t, part_i, gsum_t, gsum_i, grad_at, gpre,
@@ -103,6 +104,15 @@
         q = lax.rem(role + d, 8)
         return device_of(q // 2, y, z, lax.rem(q, 2))
 
+    loads = [
+        pltpu.make_async_copy(src, dst, in_sem.at[k])
+        for k, (src, dst) in enumerate(
+            ((w1_hbm, w1_ref), (w2_hbm, w2_ref), (ids_hbm, ids_ref), (gain_hbm, gain_ref), (x_hbm, x_ref))
+        )
+    ]
+    for load in loads:
+        load.start()
+
     barrier = pltpu.get_barrier_semaphore()
     for d in range(1, N_Z):
         pl.semaphore_signal(barrier, inc=1, device_id=ring_z(d), device_id_type=MESH)
@@ -122,26 +132,11 @@
     lead = jnp.logical_and(row < MAIN, 2 * row + t == col)
     rest = jnp.logical_and(col >= 2 * MAIN, 2 * (row - 2 * z) + t == col)
     pick = jnp.where(jnp.logical_or(lead, rest), 1.0, 0.0).astype(bf16)
-    for ref, w, ex in ((w1_ref, wa, exa), (w2_ref, wb, exb)):
+    for load, ref, w, ex in ((loads[0], w1_ref, wa, exa), (loads[1], w2_ref, wb, exb)):
+        load.wait()
         own = dot_nn(pick, ref[...].reshape(68, D)).astype(bf16)
         w[gid, z] = own[:MAIN]
         ex[0] = own[MAIN:]
-
-    mask = jnp.where(is_text, jnp.where(ids_ref[...] != 0, 1.0, 0.0), 1.0)
-    count = jnp.where(is_text, jnp.sum(mask, axis=1, keepdims=True), 256.0)
-    slot = lax.broadcasted_iota(jnp.int32, (SEG, ROWS), 0)
-    at = lax.broadcasted_iota(jnp.int32, (SEG, ROWS), 1)
-    spread = jnp.where(lax.rem(at, SEG) == slot, 1.0, 0.0).astype(bf16)
-    wide = dot_nn(mask.astype(bf16), spread)
-    segment = lax.broadcasted_iota(jnp.int32, (8, ROWS), 0)
-    at = lax.broadcasted_iota(jnp.int32, (8, ROWS), 1)
-    pmask[...] = jnp.where(at // SEG == segment, wide, 0.0).astype(bf16)
-    rowmask[...] = lax.dot_general(
-        pmask[...], jnp.ones((8, LANES), bf16), (((0,), (0,)), ((), ())), preferred_element_type=f32
-    )
-
-    def mask_of(rows, width):
-        return jnp.concatenate([rowmask[rows, :]] * (width // LANES), axis=1)
 
     pl.semaphore_wait(barrier, jnp.where(role == 0, 20, 21))
 
@@ -261,11 +256,6 @@
         arrived(e, g, recv_e.at[m, g])
         send(e, g, send_xe.at[m, dy], recv_e.at[m, g], partner)
 
-    gain = gain_ref[pl.ds(t, 1), :]
-
-    def norm_block(j):
-        standard, _ = normalise(x_ref[pl.ds(j * SEG, SEG), :])
-        normed[pl.ds(j * SEG, SEG), :] = (standard * gain).astype(bf16)
 
     def activate(width, weights, slope_at, pool_at):
         pre[:, :width] = dot_nt(normed[...], weights)
@@ -309,6 +299,10 @@
     def pool_at_e(v):
         pooled_e[...] = v
 
+    def norm_block(j):
+        standard, _ = normalise(x_ref[pl.ds(j * SEG, SEG), :])
+        normed[pl.ds(j * SEG, SEG), :] = (standard * gain).astype(bf16)
+
     steps = []
 
     def due(when, act, *args):
@@ -343,10 +337,32 @@
         for dy in y_order:
             arrived(mats[m][1], gid_of(dy, 1), recv_e.at[m, gid_of(dy, 1)])
 
+    start(0)
+    for load in loads[2:]:
+        load.wait()
+    gain = gain_ref[pl.ds(t, 1), :]
+
+    mask = jnp.where(is_text, jnp.where(ids_ref[...] != 0, 1.0, 0.0), 1.0)
+    count = jnp.where(is_text, jnp.sum(mask, axis=1, keepdims=True), 256.0)
+    slot = lax.broadcasted_iota(jnp.int32, (SEG, ROWS), 0)
+    at = lax.broadcasted_iota(jnp.int32, (SEG, ROWS), 1)
+    spread = jnp.where(lax.rem(at, SEG) == slot, 1.0, 0.0).astype(bf16)
+    wide = dot_nn(mask.astype(bf16), spread)
+    segment = lax.broadcasted_iota(jnp.int32, (8, ROWS), 0)
+    at = lax.broadcasted_iota(jnp.int32, (8, ROWS), 1)
+    pmask[...] = jnp.where(at // SEG == segment, wide, 0.0).astype(bf16)
+    rowmask[...] = lax.dot_general(
+        pmask[...], jnp.ones((8, LANES), bf16), (((0,), (0,)), ((), ())), preferred_element_type=f32
+    )
+
+    def mask_of(rows, width):
+        return jnp.concatenate([rowmask[rows, :]] * (width // LANES), axis=1)
+
     for j in range(8):
-        due(0.1 + 1.0 * j, norm_block, j)
+        due(13.0 + 1.2 * j, norm_block, j)
     for m, at in ((0, 0.0), (1, SECOND)):
-        due(at, start, m)
+        if m:
+            due(at, start, m)
         for n, d in enumerate(z_order[1:]):
             due(at + 4.4 + 1.3 * n, z_arrival, m, d)
         for n, d in enumerate(z_order):
@@ -354,22 +370,22 @@
         due(at + 5.0, back_own, m)
         due(at + 8.0, back_partner, m)
         for hop in range(1, 5):
-            due(at + 6.0 + 4.0 * hop, back_ring, m, 0, hop)
-            due(at + 9.0 + 4.0 * hop, back_ring, m, 1, hop)
+            due(at + 6.0 + 5.0 * hop, back_ring, m, 0, hop)
+            due(at + 9.0 + 5.0 * hop, back_ring, m, 1, hop)
         due(at + 6.5, extras_take, m, 0)
         due(at + 10.5, extras_take, m, 1)
         due(at + 15.5, extras_take, m, 2)
         due(at + 24.2, extras_rest, m)
         due(at + 26.0, extras_last, m)
     for n, dy in enumerate(y_order):
-        due(25.1 + 1.4 * n, group_forward, gid_of(dy))
-        due(30.6 + 1.4 * n, x_arrival, 0, dy)
-        due(30.7 + 1.4 * n, group_forward, gid_of(dy, 1))
+        due(26.1 + 1.4 * n, group_forward, gid_of(dy))
+        due(31.6 + 1.4 * n, x_arrival, 0, dy)
+        due(31.7 + 1.4 * n, group_forward, gid_of(dy, 1))
 
     def forward_e():
         activate(LANES, ea[...].reshape(LANES, D), slope_at_e, pool_at_e)
 
-    due(36.5, forward_e)
+    due(37.5, forward_e)
     for act in sorted(steps):
         act[2](*act[3])
     sums = dot_nn(pmask[...], x_ref[...])
@@ -567,6 +583,10 @@
         out_ref[rows, :] = grad[j : j + 1, :] * mask_of(rows, D) + inv_std * (
             grad_std - m1 - standard * m2
         )
+        pltpu.make_async_copy(out_ref.at[rows], out_hbm.at[rows], out_sem.at[j]).start()
+    for j in range(8):
+        rows = slice(j * SEG, (j + 1) * SEG)
+        pltpu.make_async_copy(out_ref.at[rows], out_hbm.at[rows], out_sem.at[j]).wait()
     for copy in pending:
         copy.wait_send()
 
@@ -588,15 +608,23 @@
 
 
 def body(layer_input, caption_ids, positives, ln_gain, w_first, w_second, logit_scale, logit_bias):
-    vmem = pl.BlockSpec(memory_space=pltpu.VMEM)
+    anywhere = pl.BlockSpec(memory_space=pl.ANY)
     smem = pl.BlockSpec(memory_space=pltpu.SMEM)
     dma = pltpu.SemaphoreType.DMA
     return pl.pallas_call(
         kernel,
         out_shape=jax.ShapeDtypeStruct((ROWS, D), f32),
-        in_specs=[vmem] * 5 + [smem] * 3,
-        out_specs=vmem,
+        in_specs=[anywhere] * 5 + [smem] * 3,
+        out_specs=anywhere,
         scratch_shapes=[
+            pltpu.VMEM((ROWS, D), bf16),
+            pltpu.VMEM((8, SEG), jnp.int32),
+            pltpu.VMEM((2, D), f32),
+            pltpu.VMEM((34, 2, D), bf16),
+            pltpu.VMEM((34, 2, D), bf16),
+            pltpu.VMEM((ROWS, D), f32),
+            dma((5,)),
+            dma((8,)),
             pltpu.VMEM((8, N_Z, MAIN, D), bf16),
             pltpu.VMEM((8, N_Z, MAIN, D), bf16),
             pltpu.VMEM((8, EXTRA, D), bf16),

time: 114 us -> 108 us (0.947)
  Pallas kernels: 109 us -> 103 us
    pallas_call x1, Pallas kernels: 109 us -> 103 us  [body(): pl.pallas_call(kernel, out_shape=jax.ShapeDtypeStruct((ROWS, D), f32), in...]
where the time goes in v3:
time: 108 us
  Pallas kernels  103 us (95%)
  local copies, waits for them, and re-layouts  3.22 us (3%)
  between operations  1.31 us (1%)
    pallas_call x1, Pallas kernels, body(): pl.pallas_call(kernel, out_shape=jax.ShapeDtypeStruct((ROWS, D), f32), in...  103 us
    unnamed x1, local copies, waits for them, and re-layouts  3.22 us

profile of v3, /device:TPU:1, one launch (start us, length us, event | category | flops | bytes accessed | tf_op | source)
XLA Modules:
  0.0 107.8 jit_solution(5765731493912581705)
XLA Ops:
  1.3 103.2 %step.1 = f32[512,1152]{1,0:T(8,128)} custom-call(bf16[512,1152]{1,0:T(8,128)(2,1)} %x_hbm.1, s32[8,64]{1,0:T(8,128)} %ids_hbm.1, f32[2,1152]{1,0:T(2,128)} %gain_hbm.1, bf16[34,2,1152]{2,1,0:T(2,128)(2,1)} %bitcast.2, bf16[34,2,1152]{2,1,0:T(2,128)(2,1)} %bitcast.3, s32[6]{0:T(128)} %positive_ref.1, f32[1]{0:T(128)S(6)} %copy.10.scale_ref, f32[1]{0:T(128)S(6)} %copy.11.bias_ref), custom_call_target="tpu_custom_call" | custom-call | tf_op jit(solution)/shard_map/step/pallas_call | solution.py:614
  104.5 3.2 %copy.12 = f32[512,1152]{1,0:T(8,128)} copy(f32[512,1152]{1,0:T(8,128)} %step.1) | data formatting | bytes 4718592

commit v4 on v3

--- a/solution.py
+++ b/solution.py
@@ -18,7 +18,7 @@
 LANES = 128
 KEYED = D + LANES
 FRONT = 768
-SECOND = 22.0
+SECOND = 18.0
 
 norm_eps = 1e-06
 loss_scale = 128.0
@@ -176,8 +176,13 @@
         return pl.ds((1 - x_lo if other else x_lo) * N_Y, N_Y)
 
     def send_z(m):
-        for d in z_order[1:]:
+        for d in (1, 7, 2, 6):
             send(mats[m][0], (gid, z, every, front), send_zm.at[m, d - 1], recv_main.at[m, gid, z], ring_z(d))
+
+    def pass_z(m, origin, slot, places):
+        send(
+            mats[m][0], (gid, origin, every, front), send_zm.at[m, slot], recv_main.at[m, gid, origin], ring_z(places)
+        )
 
     def send_x(m, dy, d):
         g, zz = gid_of(dy), zid(d)
@@ -317,6 +322,11 @@
 
     def z_arrival(m, d):
         take(m, 0, 0, d)
+        if d == 2:
+            pass_z(m, zid(2), 2, -1)
+        if d == 6:
+            pass_z(m, zid(6), 4, 1)
+            pass_z(m, lax.rem(z - 2 * long + 2 * N_Z, N_Z), 3, 2 * long)
         send_y(m, d)
         send_x(m, 0, d)
 
@@ -364,7 +374,7 @@
         if m:
             due(at, start, m)
         for n, d in enumerate(z_order[1:]):
-            due(at + 4.4 + 1.3 * n, z_arrival, m, d)
+            due(at + 3.8 + 0.9 * n + (2.0 if n > 3 else 0.0), z_arrival, m, d)
         for n, d in enumerate(z_order):
             due(at + 7.0 + 2.3 * n, y_arrival, m, d)
         due(at + 5.0, back_own, m)

time: 108 us -> 101 us (0.935)
  Pallas kernels: 103 us -> 96.5 us
    pallas_call x1, Pallas kernels: 103 us -> 96.5 us  [body(): pl.pallas_call(kernel, out_shape=jax.ShapeDtypeStruct((ROWS, D), f32), in...]
where the time goes in v4:
time: 101 us
  Pallas kernels  96.5 us (96%)
  local copies, waits for them, and re-layouts  3.22 us (3%)
  between operations  1.31 us (1%)
    pallas_call x1, Pallas kernels, body(): pl.pallas_call(kernel, out_shape=jax.ShapeDtypeStruct((ROWS, D), f32), in...  96.5 us
    unnamed x1, local copies, waits for them, and re-layouts  3.22 us

profile of v4, /device:TPU:1, one launch (start us, length us, event | category | flops | bytes accessed | tf_op | source)
XLA Modules:
  0.0 101.0 jit_solution(7934872579175040981)
XLA Ops:
  1.3 96.5 %step.1 = f32[512,1152]{1,0:T(8,128)} custom-call(bf16[512,1152]{1,0:T(8,128)(2,1)} %x_hbm.1, s32[8,64]{1,0:T(8,128)} %ids_hbm.1, f32[2,1152]{1,0:T(2,128)} %gain_hbm.1, bf16[34,2,1152]{2,1,0:T(2,128)(2,1)} %bitcast.2, bf16[34,2,1152]{2,1,0:T(2,128)(2,1)} %bitcast.3, s32[6]{0:T(128)} %positive_ref.1, f32[1]{0:T(128)S(6)} %copy.10.scale_ref, f32[1]{0:T(128)S(6)} %copy.11.bias_ref), custom_call_target="tpu_custom_call" | custom-call | tf_op jit(solution)/shard_map/step/pallas_call | solution.py:624
  97.8 3.2 %copy.12 = f32[512,1152]{1,0:T(8,128)} copy(f32[512,1152]{1,0:T(8,128)} %step.1) | data formatting | bytes 4718592
